TPU v7x, 32 devices: a whole 2x2x4 slice. The times are simulated.
32 devices in a mesh: tm: 4 (over y, x), space: 8 (over z, core).
Axes of the slice: x: 2, y: 2, z: 4, core: 2. Of those that a mesh axis runs over, the one named last changes fastest.
Arguments:
- latent_clip: bfloat16 [8, 16, 32, 256], P('tm', 'space'), may hold values from -45 to 45
- cotangent: bfloat16 [8, 16, 32, 128], P('tm', 'space'), may hold values from -6 to 6
- conv_weight: bfloat16 [6912, 128], replicated, may hold values from -0.078125 to 0.078125
- norm_gain: float32 [256], replicated, may hold values from 0.5 to 1.5
- norm_shift: float32 [256], replicated, may hold values from -2 to 2
Outputs:
- clip_grad: bfloat16 [8, 16, 32, 256], P('tm', 'space')
- weight_grad: float32 [6912, 128], P('space')
- gain_grad: float32 [256], replicated
- shift_grad: float32 [256], replicated
All inputs are finite; a program needn't handle non-finite values.
Results may differ from a plain program's by a relative error of at most 0.0029.
Values may be sent and summed in bfloat16 or wider, within the bound.
A program may use at most 64 MiB of HBM per device.

v0:
```python
import jax
import jax.numpy as jnp
from jax import lax
from jax.sharding import PartitionSpec as P

GROUPS = 32


def shifted(value, axis, steps):
    count = lax.axis_size(axis)
    leading, last = (max(0, -steps), min(count, count - steps))
    return lax.ppermute(value, axis, [(source, source + steps) for source in range(leading, last)])


def extended_2(block, sides, width):
    for axis, dim in sides:
        count = lax.axis_size(axis)
        forward = [(i, i + 1) for i in range(count - 1)]
        backward = [(target, source) for source, target in forward]
        low = lax.ppermute(
            lax.slice_in_dim(block, block.shape[dim] - width, None, axis=dim), axis, forward
        )
        high = lax.ppermute(lax.slice_in_dim(block, 0, width, axis=dim), axis, backward)
        block = jnp.concatenate([low, block, high], axis=dim)
    return block


def silu_slope(activation):
    sigma = jax.nn.sigmoid(activation)
    return sigma * (1.0 + activation * (1.0 - sigma))


def tap_block(source, anchors, frame_count, row_count, col_count):
    pieces = [
        source[
            anchor[0] : anchor[0] + frame_count,
            anchor[1] : anchor[1] + row_count,
            anchor[2] : anchor[2] + col_count,
            :,
        ]
        for anchor in anchors
    ]
    merged = jnp.concatenate(pieces, axis=-1)
    return merged.reshape(frame_count * row_count * col_count, merged.shape[-1])


def transposed(grad_pad, conv_weight, frame_count, row_count, col_count):
    out_channels = conv_weight.shape[1]
    channels = conv_weight.shape[0] // 27
    kernel = conv_weight.reshape(3, 3, 3, channels, out_channels)
    total = jnp.zeros((frame_count * row_count * col_count, channels), jnp.float32)
    for tap_time in range(3):
        anchors = [
            (2 - tap_time, 2 - tap_row, 2 - tap_col) for tap_row in range(3) for tap_col in range(3)
        ]
        tap_cols = tap_block(grad_pad, anchors, frame_count, row_count, col_count)
        flipped = jnp.transpose(kernel[tap_time], (0, 1, 3, 2)).reshape(9 * out_channels, channels)
        total = total + jnp.dot(tap_cols, flipped, preferred_element_type=jnp.float32)
    return total.reshape(frame_count, row_count, col_count, channels)


def shards(latent_clip, cotangent, conv_weight, norm_gain, norm_shift):
    frame_count, row_count, col_count, channels = latent_clip.shape
    out_channels = cotangent.shape[-1]
    width_group = channels // GROUPS
    tm_size = lax.axis_size("tm")
    space_size = lax.axis_size("space")
    group_count = frame_count * row_count * col_count * width_group * tm_size * space_size
    values = latent_clip.astype(jnp.float32).reshape(
        frame_count, row_count, col_count, GROUPS, width_group
    )
    group_mean = lax.psum(jnp.sum(values, axis=(0, 1, 2, 4)), ("tm", "space")) / group_count
    centered = values - group_mean[:, None]
    group_var = (
        lax.psum(jnp.sum(centered * centered, axis=(0, 1, 2, 4)), ("tm", "space")) / group_count
    )
    inv_std = lax.rsqrt(group_var + 1e-06)
    normed = (centered * inv_std[:, None]).reshape(frame_count, row_count, col_count, channels)
    activation = normed * norm_gain + norm_shift
    hidden = jax.nn.silu(activation).astype(jnp.bfloat16)
    ahead = shifted(cotangent, "tm", -1)
    time_source = jnp.concatenate([cotangent, ahead], axis=0)
    time_pad = (0, 0)
    cached = shifted(hidden, "tm", 1)
    extended = jnp.concatenate([cached, hidden], axis=0)
    rimmed = extended_2(extended, (("space", 1),), 1)
    padded = jnp.pad(rimmed, ((0, 0), (0, 0), (1, 1), (0, 0)))
    cell_count = frame_count * row_count * col_count
    upstream = cotangent.reshape(cell_count, out_channels)
    tap_grads = []
    for tap_time in range(3):
        anchors = [(tap_time, tap_row, tap_col) for tap_row in range(3) for tap_col in range(3)]
        tap_cols = tap_block(padded, anchors, frame_count, row_count, col_count)
        tap_grads.append(
            lax.dot_general(
                tap_cols, upstream, (((0,), (0,)), ((), ())), preferred_element_type=jnp.float32
            )
        )
    local_grad = jnp.concatenate(tap_grads, axis=0)
    space_shard = lax.psum_scatter(local_grad, "space", scatter_dimension=0, tiled=True)
    weight_grad = lax.psum(space_shard, "tm")
    grad_pad = jnp.pad(time_source, (time_pad, (2, 2), (1, 1), (0, 0)))
    spread = transposed(grad_pad, conv_weight, frame_count, row_count + 2, col_count)
    from_below = shifted(spread[:, 0], "space", -1)
    from_above = shifted(spread[:, row_count + 1], "space", 1)
    inner = spread[:, 1 : row_count + 1]
    inner = inner.at[:, row_count - 1].add(from_below)
    inner = inner.at[:, 0].add(from_above)
    activation_grad = inner * silu_slope(activation)
    gain_grad, shift_grad = lax.psum(
        (
            jnp.sum(activation_grad * normed, axis=(0, 1, 2)),
            jnp.sum(activation_grad, axis=(0, 1, 2)),
        ),
        ("tm", "space"),
    )
    first = jnp.sum((norm_gain * shift_grad).reshape(GROUPS, width_group), axis=1)
    second = jnp.sum((norm_gain * gain_grad).reshape(GROUPS, width_group), axis=1)
    scaled = (activation_grad * norm_gain).reshape(
        frame_count, row_count, col_count, GROUPS, width_group
    )
    normed_groups = normed.reshape(frame_count, row_count, col_count, GROUPS, width_group)
    clip_grad = inv_std[:, None] * (
        scaled - first[:, None] / group_count - normed_groups * second[:, None] / group_count
    )
    clip_grad = clip_grad.reshape(frame_count, row_count, col_count, channels).astype(jnp.bfloat16)
    return (clip_grad, weight_grad, gain_grad, shift_grad)


def solution(mesh):
    return jax.shard_map(
        shards,
        mesh=mesh,
        in_specs=(P("tm", "space", None, None), P("tm", "space", None, None), P(), P(), P()),
        out_specs=(P("tm", "space", None, None), P("space", None), P(), P()),
        check_vma=False,
    )
```

profile of v0, /device:TPU:0, one launch (start us, length us, event | category | flops | bytes accessed | tf_op | source)
XLA Modules:
  0.0 225.5 jit_solution(13261450040164895884)
XLA Ops:
  7.2 0.0 reduce-scatter.2.cloned.1.call-start
  7.2 0.9 convert_reduce_fusion
  8.1 0.1 reduce_sum.69
  8.2 0.1 reduce_sum.70
  8.3 1.3 collective-permute-start
  9.6 43.2 %psum.35 = f32[32]{0:T(128)S(1)} all-reduce(f32[32]{0:T(128)S(1)} %reduce_sum.70), channel_id=1, replica_groups=mesh['tm'=4,'space'=8] {'tm','space'}, use_global_device_ids=true, to_apply=%region_2.0 | all-reduce | flops 32 | bytes 256 | tf_op jit(solution)/shard_map/psum | solution.py:72
  52.8 0.1 sub.35
  52.8 0.1 sub.36
  52.9 0.9 fusion.33
  53.8 0.1 reduce_sum.72
  53.9 0.1 reduce_sum.73
  54.0 1.5 fusion.40
  55.6 41.0 %psum.36 = f32[32]{0:T(128)S(1)} all-reduce(f32[32]{0:T(128)S(1)} %reduce_sum.73), channel_id=1, replica_groups=mesh['tm'=4,'space'=8] {'tm','space'}, use_global_device_ids=true, to_apply=%region_5.6 | all-reduce | flops 32 | bytes 256 | tf_op jit(solution)/shard_map/psum | solution.py:75
  96.6 0.2 copy.15
  96.8 0.0 copy-start.1
  96.8 0.2 copy.13
  97.1 0.2 copy.14
  97.3 0.2 copy-done.1
  97.7 0.1 constant_dynamic-update-slice_fusion.25
  97.7 0.1 constant_dynamic-update-slice_fusion.24
  97.8 0.1 constant_dynamic-update-slice_fusion.23
  97.9 0.1 constant_dynamic-update-slice_fusion.22
  98.0 0.1 constant_dynamic-update-slice_fusion.21
  98.0 0.1 constant_dynamic-update-slice_fusion.20
  98.1 0.1 constant_dynamic-update-slice_fusion.19
  98.2 0.1 constant_dynamic-update-slice_fusion.18
  98.3 0.3 fusion.42
  98.6 0.3 convolution_add_fusion.1
  99.0 0.0 copy-start
  99.0 0.0 copy-start.2
  99.0 0.0 copy-start.3
  99.0 0.3 convolution_add_fusion
  99.4 1.3 collective-permute-start.1
  100.7 0.1 mul.75
  100.8 0.1 mul.76
  100.9 3.0 %collective-permute-start.2 = (f32[2,32,256]{2,1,0:T(8,128)S(1)}, f32[2,32,256]{2,1,0:T(8,128)S(1)}, u32[]{:S(2)}, u32[]{:S(2)}) collective-permute-start(f32[2,32,256]{2,1,0:T(8,128)S(1)} %get-tuple-element.53), channel_id=1, source_target_pairs={{0,1},{1,2},{2,3},{3,4},{4,5},{5,6},{6,7},{8,9},{9,10},{10,11},{11... | collective-permute-start | bytes 196616 | tf_op jit(solution)/shard_map/ppermute | solution.py:12
  103.9 0.9 collective-permute-done.2
  104.8 0.1 fusion.38
  105.0 4.2 %collective-permute-start.3 = (bf16[2,2,32,256]{3,2,1,0:T(8,128)(2,1)S(1)}, bf16[2,2,32,256]{3,2,1,0:T(8,128)(2,1)S(1)}, u32[]{:S(2)}, u32[]{:S(2)}) collective-permute-start(bf16[2,2,32,256]{3,2,1,0:T(8,128)(2,1)S(1)} %get-tuple-element.90), channel_id=1, source_target_pairs={{0,8},{8,16},{16,24},{1,9},{9,17},{17,25},{2,10},{10,18},{18,26},{... | collective-permute-start | bytes 196616 | tf_op jit(solution)/shard_map/ppermute | solution.py:12
  109.1 1.9 collective-permute-done.3
  111.1 1.4 collective-permute-start.4
  112.6 1.3 collective-permute-start.5
  113.9 4.6 %collective-permute-done.5 = bf16[4,1,32,256]{3,2,1,0:T(8,128)(2,1)S(1)} collective-permute-done((bf16[4,1,32,256]{3,2,1,0:T(8,128)(2,1)S(1)}, bf16[4,1,32,256]{3,2,1,0:T(8,128)(2,1)S(1)}, u32[]{:S(2)}, u32[]{:S(2)}) %collective-permute-start.5) | collective-permute-done | bytes 65568 | tf_op jit(solution)/shard_map/ppermute | solution.py:23
  118.4 0.1 select_maximum_fusion
  118.9 0.3 convolution_bitcast_fusion
  119.2 0.3 convolution_bitcast_fusion.2
  119.6 0.3 convolution_bitcast_fusion.1
  119.9 2.0 pad_maximum_fusion
  121.9 0.0 reduce-scatter.2.cloned.1.call-update
  122.0 0.0 all-reduce.5.cloned.1.call-start
  122.0 45.1 %all-reduce.2 = (f32[256]{0:T(256)S(1)}, f32[256]{0:T(256)S(1)}) all-reduce(f32[256]{0:T(256)S(1)} %get-tuple-element.29, f32[256]{0:T(256)S(1)} %get-tuple-element.28), channel_id=1, replica_groups=mesh['tm'=4,'space'=8] {'tm','space'}, use_global_device_ids=true, to_apply=%region_10.11 | all-reduce | flops 512 | bytes 4096 | tf_op jit(solution)/shard_map/psum | solution.py:110
  167.2 0.1 reshape.151
  167.2 0.1 reduce_sum.75
  167.4 3.1 %reduce-scatter.2.cloned.1.call-done = f32[864,128]{1,0:T(8,128)} async-done(((f32[6912,128]{1,0:T(8,128)}), f32[864,128]{1,0:T(8,128)}) %reduce-scatter.2.cloned.1.call-update) | async-done | bytes 442384 | tf_op jit(solution)/shard_map/reduce_scatter | solution.py:100
  170.5 0.0 all-reduce.5.cloned.1.call-update
  170.5 0.1 sub.40
  170.6 0.1 sub.41
  170.7 0.1 reshape.152
  170.8 0.1 reduce_sum.77
  170.9 0.1 mul.88
  171.0 0.1 mul.89
  171.1 0.7 fusion.32
  171.8 45.1 %all-reduce.5.cloned.1.call-done = f32[864,128]{1,0:T(8,128)} async-done(((f32[864,128]{1,0:T(8,128)}), f32[864,128]{1,0:T(8,128)}) %all-reduce.5.cloned.1.call-update) | async-done | bytes 442384 | tf_op jit(solution)/shard_map/psum | solution.py:101
  216.9 1.8 copy.74
  (35 shorter events, 0.4 us)
Async XLA Ops:
  7.2 163.3 %reduce-scatter.2.cloned.1.call-start = ((), (), s32[]{:S(2)}) async-start(), calls=%async_computation.1 | async-start | bytes 3981312 | tf_op jit(solution)/shard_map/reduce_scatter | solution.py:100
  8.3 89.0 %collective-permute-start = (bf16[2,2,32,128]{3,2,1,0:T(8,128)(2,1)}, bf16[2,2,32,128]{3,2,1,0:T(8,128)(2,1)S(1)}, u32[]{:S(2)}, u32[]{:S(2)}) collective-permute-start(bf16[2,2,32,128]{3,2,1,0:T(8,128)(2,1)} %param.10), channel_id=1, source_target_pairs={{8,0},{16,8},{24,16},{9,1},{17,9},{25,17},{10,2},{18,10},{26,18},{... | collective-permute-start | bytes 98312 | tf_op jit(solution)/shard_map/ppermute | solution.py:12
  96.8 0.8 copy-start.1
  99.0 5.8 %copy-start = (bf16[2,2,32,256]{3,2,1,0:T(8,128)(2,1)S(1)}, bf16[2,2,32,256]{3,2,1,0:T(8,128)(2,1)}, u32[]{:S(2)}) copy-start(bf16[2,2,32,256]{3,2,1,0:T(8,128)(2,1)} %param.9) | copy-start | bytes 196612
  99.0 5.8 %copy-start.2 = (f32[256]{0:T(256)S(1)}, f32[256]{0:T(256)}, u32[]{:S(2)}) copy-start(f32[256]{0:T(256)} %param.12) | copy-start | bytes 3076
  99.0 5.8 %copy-start.3 = (f32[256]{0:T(256)S(1)}, f32[256]{0:T(256)}, u32[]{:S(2)}) copy-start(f32[256]{0:T(256)} %param.13) | copy-start | bytes 3076
  99.4 4.5 %collective-permute-start.1 = (f32[2,32,256]{2,1,0:T(8,128)S(1)}, f32[2,32,256]{2,1,0:T(8,128)S(1)}, u32[]{:S(2)}, u32[]{:S(2)}) collective-permute-start(f32[2,32,256]{2,1,0:T(8,128)S(1)} %get-tuple-element.54), channel_id=1, source_target_pairs={{1,0},{2,1},{3,2},{4,3},{5,4},{6,5},{7,6},{9,8},{10,9},{11,10},{12... | collective-permute-start | bytes 196616 | tf_op jit(solution)/shard_map/ppermute | solution.py:12
  100.9 3.9 %collective-permute-start.2 = (f32[2,32,256]{2,1,0:T(8,128)S(1)}, f32[2,32,256]{2,1,0:T(8,128)S(1)}, u32[]{:S(2)}, u32[]{:S(2)}) collective-permute-start(f32[2,32,256]{2,1,0:T(8,128)S(1)} %get-tuple-element.53), channel_id=1, source_target_pairs={{0,1},{1,2},{2,3},{3,4},{4,5},{5,6},{6,7},{8,9},{9,10},{10,11},{11... | collective-permute-start | bytes 196616 | tf_op jit(solution)/shard_map/ppermute | solution.py:12
  105.0 6.1 %collective-permute-start.3 = (bf16[2,2,32,256]{3,2,1,0:T(8,128)(2,1)S(1)}, bf16[2,2,32,256]{3,2,1,0:T(8,128)(2,1)S(1)}, u32[]{:S(2)}, u32[]{:S(2)}) collective-permute-start(bf16[2,2,32,256]{3,2,1,0:T(8,128)(2,1)S(1)} %get-tuple-element.90), channel_id=1, source_target_pairs={{0,8},{8,16},{16,24},{1,9},{9,17},{17,25},{2,10},{10,18},{18,26},{... | collective-permute-start | bytes 196616 | tf_op jit(solution)/shard_map/ppermute | solution.py:12
  111.1 2.8 %collective-permute-start.4 = (bf16[4,1,32,256]{3,2,1,0:T(8,128)(2,1)S(1)}, bf16[4,1,32,256]{3,2,1,0:T(8,128)(2,1)S(1)}, u32[]{:S(2)}, u32[]{:S(2)}) collective-permute-start(bf16[4,1,32,256]{3,2,1,0:T(8,128)(2,1)S(1)} %get-tuple-element.88), channel_id=1, source_target_pairs={{0,1},{1,2},{2,3},{3,4},{4,5},{5,6},{6,7},{8,9},{9,10},{10,11},{11... | collective-permute-start | bytes 196616 | tf_op jit(solution)/shard_map/ppermute | solution.py:20
  112.6 5.9 %collective-permute-start.5 = (bf16[4,1,32,256]{3,2,1,0:T(8,128)(2,1)S(1)}, bf16[4,1,32,256]{3,2,1,0:T(8,128)(2,1)S(1)}, u32[]{:S(2)}, u32[]{:S(2)}) collective-permute-start(bf16[4,1,32,256]{3,2,1,0:T(8,128)(2,1)S(1)} %get-tuple-element.89), channel_id=1, source_target_pairs={{1,0},{2,1},{3,2},{4,3},{5,4},{6,5},{7,6},{9,8},{10,9},{11,10},{12... | collective-permute-start | bytes 196616 | tf_op jit(solution)/shard_map/ppermute | solution.py:23
  122.0 94.9 %all-reduce.5.cloned.1.call-start = ((), (), s32[]{:S(2)}) async-start(), calls=%async_computation.2 | async-start | bytes 884736 | tf_op jit(solution)/shard_map/psum | solution.py:101
  167.2 51.5 %copy-start.4 = (f32[256]{0:T(256)}, f32[256]{0:T(256)S(1)}, u32[]{:S(2)}) copy-start(f32[256]{0:T(256)S(1)} %get-tuple-element.97) | copy-start | bytes 3076
  167.2 51.5 %copy-start.5 = (f32[256]{0:T(256)}, f32[256]{0:T(256)S(1)}, u32[]{:S(2)}) copy-start(f32[256]{0:T(256)S(1)} %get-tuple-element.98) | copy-start | bytes 3076
Sparse Core Ops, SparseCore 0:
  122.1 48.3 reduce-scatter.1
  173.8 43.0 all-reduce.4
where the time goes:
time: 226 us
  blocking collectives  129 us (57%)
  waiting for transfers between devices  55.6 us (25%)
  between operations  14.5 us (6%)
  starting transfers between devices  12.6 us (6%)
  local copies, waits for them, and re-layouts  6.15 us (3%)
  other arithmetic  5.25 us (2%)
    psum x1, blocking collectives, shards(): lax.psum((jnp.sum(activation_grad * normed, axis=(0, 1, 2)), jnp.sum(acti...  45.1 us
    psum x1, waiting for transfers between devices, shards(): weight_grad = lax.psum(space_shard, 'tm')  45.1 us
    psum x1, blocking collectives, shards(): lax.psum(jnp.sum(values, axis=(0, 1, 2, 4)), ('tm', 'space')) / group_count  43.2 us
    psum x1, blocking collectives, shards(): lax.psum(jnp.sum(centered * centered, axis=(0, 1, 2, 4)), ('tm', 'space'))  41 us
    ppermute x4, starting transfers between devices, shifted(): lax.ppermute(value, axis, [(source, source + steps) for source in range(l...  9.8 us
    ppermute x1, waiting for transfers between devices, extended_2(): lax.ppermute(lax.slice_in_dim(block, 0, width, axis=dim), axis, backward)  4.55 us
  transfers between devices with their start and end apart: 8, of which 5 were waited for; matrix products, arithmetic and copies ran while one was open for 2% of the time, Pallas kernels for 0%

commit v1 on v0

--- a/solution.py
+++ b/solution.py
@@ -98,7 +98,21 @@
         )
     local_grad = jnp.concatenate(tap_grads, axis=0)
     space_shard = lax.psum_scatter(local_grad, "space", scatter_dimension=0, tiled=True)
-    weight_grad = lax.psum(space_shard, "tm")
+
+    def halves_map(my_data):
+        mesh_dim = "tm"
+        axis_len = lax.axis_size(mesh_dim)
+        all_rows = my_data
+        for no in [ii for ii in (1, 2, 4, 8, 16) if ii < axis_len]:
+            pool = []
+            dev_j = 0
+            while dev_j < axis_len:
+                pool.append((dev_j, dev_j ^ no))
+                dev_j += 1
+            all_rows = all_rows + lax.ppermute(all_rows, mesh_dim, pool)
+        return all_rows
+
+    weight_grad = halves_map(space_shard)
     grad_pad = jnp.pad(time_source, (time_pad, (2, 2), (1, 1), (0, 0)))
     spread = transposed(grad_pad, conv_weight, frame_count, row_count + 2, col_count)
     from_below = shifted(spread[:, 0], "space", -1)

time: 226 us -> 235 us (1.040)
  waiting for transfers between devices: 55.6 us -> 62.4 us
  starting transfers between devices: 12.6 us -> 16.4 us
    psum x1 -> x0, waiting for transfers between devices: 45.1 us -> none  [shards(): weight_grad = lax.psum(space_shard, 'tm')]
    reduce_scatter x1, waiting for transfers between devices: 3.13 us -> 47.5 us  [shards(): lax.psum_scatter(local_grad, 'space', scatter_dimension=0, tiled=True)]
    ppermute x0 -> x2, waiting for transfers between devices: none -> 7.6 us  [halves_map(): all_rows = all_rows + lax.ppermute(all_rows, mesh_dim, pool)]
    ppermute x0 -> x2, starting transfers between devices: none -> 3.83 us  [halves_map(): all_rows = all_rows + lax.ppermute(all_rows, mesh_dim, pool)]
  transfers between devices with their start and end apart: 8 -> 9, of which waited for: 5 -> 5; matrix products, arithmetic and copies ran while one was open for 2% -> 2% of each run, Pallas kernels for 0% -> 0%
where the time goes in v1:
time: 235 us; the launch traced here: 234 us
  blocking collectives  127 us (54%)
  waiting for transfers between devices  62.4 us (27%)
  starting transfers between devices  16.4 us (7%)
  between operations  14.5 us (6%)
  other arithmetic  7.11 us (3%)
  local copies, waits for them, and re-layouts  4.35 us (2%)
    reduce_scatter x1, waiting for transfers between devices, shards(): lax.psum_scatter(local_grad, 'space', scatter_dimension=0, tiled=True)  47.5 us
    psum x1, blocking collectives, shards(): lax.psum(jnp.sum(values, axis=(0, 1, 2, 4)), ('tm', 'space')) / group_count  43.2 us
    psum x1, blocking collectives, shards(): lax.psum((jnp.sum(activation_grad * normed, axis=(0, 1, 2)), jnp.sum(acti...  43 us
    psum x1, blocking collectives, shards(): lax.psum(jnp.sum(centered * centered, axis=(0, 1, 2, 4)), ('tm', 'space'))  41 us
    ppermute x4, starting transfers between devices, shifted(): lax.ppermute(value, axis, [(source, source + steps) for source in range(l...  9.8 us
    ppermute x2, waiting for transfers between devices, halves_map(): all_rows = all_rows + lax.ppermute(all_rows, mesh_dim, pool)  7.6 us
  transfers between devices with their start and end apart: 9, of which 5 were waited for; matrix products, arithmetic and copies ran while one was open for 2% of the time, Pallas kernels for 0%

profile of v1, /device:TPU:0, one launch (start us, length us, event | category | flops | bytes accessed | tf_op | source)
XLA Modules:
  0.0 234.0 jit_solution(17456278367312747065)
XLA Ops:
  7.2 0.0 reduce-scatter.2.cloned.1.call-start
  7.2 0.9 convert_reduce_fusion
  8.1 0.1 reduce_sum.69
  8.2 0.1 reduce_sum.70
  8.3 1.3 collective-permute-start
  9.6 43.2 %psum.28 = f32[32]{0:T(128)S(1)} all-reduce(f32[32]{0:T(128)S(1)} %reduce_sum.70), channel_id=1, replica_groups=mesh['tm'=4,'space'=8] {'tm','space'}, use_global_device_ids=true, to_apply=%region_2.0 | all-reduce | flops 32 | bytes 256 | tf_op jit(solution)/shard_map/psum | solution.py:72
  52.8 0.1 sub.35
  52.8 0.1 sub.36
  52.9 0.9 fusion.33
  53.8 0.1 reduce_sum.72
  53.9 0.1 reduce_sum.73
  54.0 1.5 fusion.40
  55.6 41.0 %psum.29 = f32[32]{0:T(128)S(1)} all-reduce(f32[32]{0:T(128)S(1)} %reduce_sum.73), channel_id=1, replica_groups=mesh['tm'=4,'space'=8] {'tm','space'}, use_global_device_ids=true, to_apply=%region_5.6 | all-reduce | flops 32 | bytes 256 | tf_op jit(solution)/shard_map/psum | solution.py:75
  96.6 0.2 copy.15
  96.8 0.0 copy-start.1
  96.9 0.2 copy.13
  97.1 0.2 copy.14
  97.4 0.2 copy-done.1
  97.7 0.1 constant_dynamic-update-slice_fusion.25
  97.8 0.1 constant_dynamic-update-slice_fusion.24
  97.8 0.1 constant_dynamic-update-slice_fusion.23
  97.9 0.1 constant_dynamic-update-slice_fusion.22
  98.0 0.1 constant_dynamic-update-slice_fusion.21
  98.1 0.1 constant_dynamic-update-slice_fusion.20
  98.1 0.1 constant_dynamic-update-slice_fusion.19
  98.2 0.1 constant_dynamic-update-slice_fusion.18
  98.3 0.3 fusion.42
  98.6 0.3 convolution_add_fusion.1
  99.0 0.0 copy-start
  99.0 0.0 copy-start.3
  99.0 0.3 convolution_add_fusion
  99.4 1.3 collective-permute-start.1
  100.7 0.1 mul.75
  100.8 0.1 mul.76
  100.9 3.0 %collective-permute-start.2 = (f32[2,32,256]{2,1,0:T(8,128)S(1)}, f32[2,32,256]{2,1,0:T(8,128)S(1)}, u32[]{:S(2)}, u32[]{:S(2)}) collective-permute-start(f32[2,32,256]{2,1,0:T(8,128)S(1)} %get-tuple-element.53), channel_id=1, source_target_pairs={{0,1},{1,2},{2,3},{3,4},{4,5},{5,6},{6,7},{8,9},{9,10},{10,11},{11... | collective-permute-start | bytes 196616 | tf_op jit(solution)/shard_map/ppermute | solution.py:12
  104.0 0.9 collective-permute-done.2
  104.9 0.1 fusion.38
  105.0 4.2 %collective-permute-start.3 = (bf16[2,2,32,256]{3,2,1,0:T(8,128)(2,1)S(1)}, bf16[2,2,32,256]{3,2,1,0:T(8,128)(2,1)S(1)}, u32[]{:S(2)}, u32[]{:S(2)}) collective-permute-start(bf16[2,2,32,256]{3,2,1,0:T(8,128)(2,1)S(1)} %get-tuple-element.90), channel_id=1, source_target_pairs={{0,8},{8,16},{16,24},{1,9},{9,17},{17,25},{2,10},{10,18},{18,26},{... | collective-permute-start | bytes 196616 | tf_op jit(solution)/shard_map/ppermute | solution.py:12
  109.2 1.9 collective-permute-done.3
  111.1 1.4 collective-permute-start.4
  112.6 1.3 collective-permute-start.5
  113.9 4.6 %collective-permute-done.5 = bf16[4,1,32,256]{3,2,1,0:T(8,128)(2,1)S(1)} collective-permute-done((bf16[4,1,32,256]{3,2,1,0:T(8,128)(2,1)S(1)}, bf16[4,1,32,256]{3,2,1,0:T(8,128)(2,1)S(1)}, u32[]{:S(2)}, u32[]{:S(2)}) %collective-permute-start.5) | collective-permute-done | bytes 65568 | tf_op jit(solution)/shard_map/ppermute | solution.py:23
  118.4 0.1 select_maximum_fusion
  118.9 0.3 convolution_bitcast_fusion
  119.3 0.3 convolution_bitcast_fusion.2
  119.6 0.3 convolution_bitcast_fusion.1
  120.0 2.0 pad_maximum_fusion
  121.9 0.0 reduce-scatter.2.cloned.1.call-update
  122.0 47.5 %reduce-scatter.2.cloned.1.call-done = f32[864,128]{1,0:T(8,128)} async-done(((f32[6912,128]{1,0:T(8,128)}), f32[864,128]{1,0:T(8,128)}) %reduce-scatter.2.cloned.1.call-update) | async-done | bytes 442384 | tf_op jit(solution)/shard_map/reduce_scatter | solution.py:100
  169.4 1.5 collective-permute-start.6
  170.9 43.0 %all-reduce.2 = (f32[256]{0:T(256)S(1)}, f32[256]{0:T(256)S(1)}) all-reduce(f32[256]{0:T(256)S(1)} %get-tuple-element.29, f32[256]{0:T(256)S(1)} %get-tuple-element.28), channel_id=1, replica_groups=mesh['tm'=4,'space'=8] {'tm','space'}, use_global_device_ids=true, to_apply=%region_10.11 | all-reduce | flops 512 | bytes 4096 | tf_op jit(solution)/shard_map/psum | solution.py:124
  213.9 0.1 reshape.151
  214.0 0.1 reduce_sum.75
  214.1 1.1 add.72
  215.2 2.3 collective-permute-start.7
  217.5 0.1 sub.40
  217.6 0.1 sub.41
  217.7 0.1 reshape.152
  217.8 0.1 reduce_sum.77
  217.9 0.1 mul.88
  218.0 0.1 mul.89
  218.1 0.7 fusion.32
  218.8 7.6 %collective-permute-done.7 = f32[864,128]{1,0:T(8,128)S(1)} collective-permute-done((f32[864,128]{1,0:T(8,128)S(1)}, f32[864,128]{1,0:T(8,128)S(1)}, u32[]{:S(2)}, u32[]{:S(2)}) %collective-permute-start.7) | collective-permute-done | bytes 442400 | tf_op jit(solution)/shard_map/ppermute | solution.py:112
  226.4 0.8 add.73
  (37 shorter events, 0.4 us)
Async XLA Ops:
  7.2 162.3 %reduce-scatter.2.cloned.1.call-start = ((), (), s32[]{:S(2)}) async-start(), calls=%async_computation.1 | async-start | bytes 3981312 | tf_op jit(solution)/shard_map/reduce_scatter | solution.py:100
  8.3 89.1 %collective-permute-start = (bf16[2,2,32,128]{3,2,1,0:T(8,128)(2,1)}, bf16[2,2,32,128]{3,2,1,0:T(8,128)(2,1)S(1)}, u32[]{:S(2)}, u32[]{:S(2)}) collective-permute-start(bf16[2,2,32,128]{3,2,1,0:T(8,128)(2,1)} %param.10), channel_id=1, source_target_pairs={{8,0},{16,8},{24,16},{9,1},{17,9},{25,17},{10,2},{18,10},{26,18},{... | collective-permute-start | bytes 98312 | tf_op jit(solution)/shard_map/ppermute | solution.py:12
  96.8 0.8 copy-start.1
  99.0 5.9 %copy-start = (bf16[2,2,32,256]{3,2,1,0:T(8,128)(2,1)S(1)}, bf16[2,2,32,256]{3,2,1,0:T(8,128)(2,1)}, u32[]{:S(2)}) copy-start(bf16[2,2,32,256]{3,2,1,0:T(8,128)(2,1)} %param.9) | copy-start | bytes 196612
  99.0 5.8 %copy-start.2 = (f32[256]{0:T(256)S(1)}, f32[256]{0:T(256)}, u32[]{:S(2)}) copy-start(f32[256]{0:T(256)} %param.12) | copy-start | bytes 3076
  99.0 5.8 %copy-start.3 = (f32[256]{0:T(256)S(1)}, f32[256]{0:T(256)}, u32[]{:S(2)}) copy-start(f32[256]{0:T(256)} %param.13) | copy-start | bytes 3076
  99.4 4.5 %collective-permute-start.1 = (f32[2,32,256]{2,1,0:T(8,128)S(1)}, f32[2,32,256]{2,1,0:T(8,128)S(1)}, u32[]{:S(2)}, u32[]{:S(2)}) collective-permute-start(f32[2,32,256]{2,1,0:T(8,128)S(1)} %get-tuple-element.54), channel_id=1, source_target_pairs={{1,0},{2,1},{3,2},{4,3},{5,4},{6,5},{7,6},{9,8},{10,9},{11,10},{12... | collective-permute-start | bytes 196616 | tf_op jit(solution)/shard_map/ppermute | solution.py:12
  100.9 3.9 %collective-permute-start.2 = (f32[2,32,256]{2,1,0:T(8,128)S(1)}, f32[2,32,256]{2,1,0:T(8,128)S(1)}, u32[]{:S(2)}, u32[]{:S(2)}) collective-permute-start(f32[2,32,256]{2,1,0:T(8,128)S(1)} %get-tuple-element.53), channel_id=1, source_target_pairs={{0,1},{1,2},{2,3},{3,4},{4,5},{5,6},{6,7},{8,9},{9,10},{10,11},{11... | collective-permute-start | bytes 196616 | tf_op jit(solution)/shard_map/ppermute | solution.py:12
  105.0 6.1 %collective-permute-start.3 = (bf16[2,2,32,256]{3,2,1,0:T(8,128)(2,1)S(1)}, bf16[2,2,32,256]{3,2,1,0:T(8,128)(2,1)S(1)}, u32[]{:S(2)}, u32[]{:S(2)}) collective-permute-start(bf16[2,2,32,256]{3,2,1,0:T(8,128)(2,1)S(1)} %get-tuple-element.90), channel_id=1, source_target_pairs={{0,8},{8,16},{16,24},{1,9},{9,17},{17,25},{2,10},{10,18},{18,26},{... | collective-permute-start | bytes 196616 | tf_op jit(solution)/shard_map/ppermute | solution.py:12
  111.1 2.8 %collective-permute-start.4 = (bf16[4,1,32,256]{3,2,1,0:T(8,128)(2,1)S(1)}, bf16[4,1,32,256]{3,2,1,0:T(8,128)(2,1)S(1)}, u32[]{:S(2)}, u32[]{:S(2)}) collective-permute-start(bf16[4,1,32,256]{3,2,1,0:T(8,128)(2,1)S(1)} %get-tuple-element.88), channel_id=1, source_target_pairs={{0,1},{1,2},{2,3},{3,4},{4,5},{5,6},{6,7},{8,9},{9,10},{10,11},{11... | collective-permute-start | bytes 196616 | tf_op jit(solution)/shard_map/ppermute | solution.py:20
  112.6 5.9 %collective-permute-start.5 = (bf16[4,1,32,256]{3,2,1,0:T(8,128)(2,1)S(1)}, bf16[4,1,32,256]{3,2,1,0:T(8,128)(2,1)S(1)}, u32[]{:S(2)}, u32[]{:S(2)}) collective-permute-start(bf16[4,1,32,256]{3,2,1,0:T(8,128)(2,1)S(1)} %get-tuple-element.89), channel_id=1, source_target_pairs={{1,0},{2,1},{3,2},{4,3},{5,4},{6,5},{7,6},{9,8},{10,9},{11,10},{12... | collective-permute-start | bytes 196616 | tf_op jit(solution)/shard_map/ppermute | solution.py:23
  169.4 44.7 %collective-permute-start.6 = (f32[864,128]{1,0:T(8,128)}, f32[864,128]{1,0:T(8,128)S(1)}, u32[]{:S(2)}, u32[]{:S(2)}) collective-permute-start(f32[864,128]{1,0:T(8,128)} %reduce-scatter.2.cloned.1.call-done), channel_id=1, source_target_pairs={{0,8},{8,0},{16,24},{24,16},{1,9},{9,1},{17,25},{25,17},{2,10},{10... | collective-permute-start | bytes 1327112 | tf_op jit(solution)/shard_map/ppermute | solution.py:112
  213.9 13.3 %copy-start.4 = (f32[256]{0:T(256)}, f32[256]{0:T(256)S(1)}, u32[]{:S(2)}) copy-start(f32[256]{0:T(256)S(1)} %get-tuple-element.30) | copy-start | bytes 3076
  213.9 13.3 %copy-start.5 = (f32[256]{0:T(256)}, f32[256]{0:T(256)S(1)}, u32[]{:S(2)}) copy-start(f32[256]{0:T(256)S(1)} %get-tuple-element.31) | copy-start | bytes 3076
  215.2 11.2 %collective-permute-start.7 = (f32[864,128]{1,0:T(8,128)S(1)}, f32[864,128]{1,0:T(8,128)S(1)}, u32[]{:S(2)}, u32[]{:S(2)}) collective-permute-start(f32[864,128]{1,0:T(8,128)S(1)} %add.72), channel_id=1, source_target_pairs={{0,16},{8,24},{16,0},{24,8},{1,17},{9,25},{17,1},{25,9},{2,18},{10... | collective-permute-start | bytes 1327112 | tf_op jit(solution)/shard_map/ppermute | solution.py:112
Sparse Core Ops, SparseCore 0:
  122.1 47.3 reduce-scatter.1
